TPU v7x, 32 devices: a whole 2x2x4 slice. The times are simulated.
32 devices in a mesh: gx: 4 (over z), gy: 2 (over y), gz: 4 (over x, core).
Axes of the slice: x: 2, y: 2, z: 4, core: 2. Of those that a mesh axis runs over, the one named last changes fastest.
Arguments:
- adjoint_fields: float32 [6, 1, 16, 16, 512], P(None, None, 'gx', 'gy', 'gz'), may hold values from -6 to 6
- forward_fields: bfloat16 [2, 3, 1, 16, 16, 512], P(None, None, None, 'gx', 'gy', 'gz'), may hold values from -6 to 6
- rock_unit: int32 [16, 16, 512], P('gx', 'gy', 'gz'), may hold values from 0 to 31
- unit_conductivity: int32 [32], replicated, may hold values from 50 to 2000
- receiver_cells: int32 [256], replicated, may hold values from 0 to 131071
- residuals: float32 [2, 1, 256], replicated, may hold values from -6 to 6
- model_vectors: float32 [16, 4, 16, 512], P('gx', None, 'gy', 'gz'), may hold values from -6 to 6
Outputs:
- adjoint_state: float32 [6, 1, 16, 16, 512], P(None, None, 'gx', 'gy', 'gz')
- normal_product: float32 [16, 4, 16, 512], P('gx', None, 'gy', 'gz')
Inputs may be any that keep to these rules, and one draw needn't show every extreme that they name: `rock_unit`: each entry is a rock unit number. `receiver_cells`: a receiver's linear cell index; two receivers may share a cell.
All inputs are finite; a program needn't handle non-finite values.
Results may differ from a plain program's by a relative error of at most 0.00075.
Values sent between devices are 32-bit elements; how exact they have to be, the bound alone decides.
A program may use at most 64 MiB of HBM per device.

v0:
```python
import math
import jax
import jax.numpy as jnp
from jax import lax
from jax.sharding import PartitionSpec as P

LOSS_FACTOR = 0.5
COURANT = 0.5


def padded_2(block, sides, width):
    for axis, dim in sides:
        count = lax.axis_size(axis)
        forward = [(i, i + 1) for i in range(count - 1)]
        backward = [(target, source) for source, target in forward]
        low = lax.ppermute(
            lax.slice_in_dim(block, block.shape[dim] - width, None, axis=dim), axis, forward
        )
        high = lax.ppermute(lax.slice_in_dim(block, 0, width, axis=dim), axis, backward)
        block = jnp.concatenate([low, block, high], axis=dim)
    return block


def crop(array, outer, inner):
    cut = outer - inner
    if cut == 0:
        return array
    return array[..., cut:-cut, cut:-cut, cut:-cut]


def local(
    adjoint_fields,
    forward_fields,
    rock_unit,
    unit_conductivity,
    receiver_cells,
    residuals,
    model_vectors,
):
    moments = forward_fields.shape[0]
    sources = adjoint_fields.shape[1]
    tile_x, tile_y, tile_z = rock_unit.shape
    whole_x = tile_x * lax.axis_size("gx")
    whole_y = tile_y * lax.axis_size("gy")
    whole_z = tile_z * lax.axis_size("gz")
    unit_count = unit_conductivity.shape[0]
    labels = lax.broadcasted_iota(jnp.int32, (unit_count, 1, 1, 1), 0)
    looked_up = jnp.sum(
        jnp.where(rock_unit[None] == labels, unit_conductivity[:, None, None, None], 0), axis=0
    )
    conductivity = looked_up.astype(jnp.float32) * 0.001
    depth = 1
    damping = LOSS_FACTOR * conductivity
    keep_ext = (1.0 - damping) / (1.0 + damping)
    drive_ext = COURANT / (1.0 + damping)
    sigma_tile = crop(conductivity, depth - 1, 0)
    anchor_x = lax.axis_index("gx") * tile_x
    anchor_y = lax.axis_index("gy") * tile_y
    anchor_z = lax.axis_index("gz") * tile_z
    coord_x = lax.broadcasted_iota(jnp.int32, (tile_x + 2 * depth, 1, 1), 0) + anchor_x - depth
    coord_y = lax.broadcasted_iota(jnp.int32, (1, tile_y + 2 * depth, 1), 1) + anchor_y - depth
    coord_z = lax.broadcasted_iota(jnp.int32, (1, 1, tile_z + 2 * depth), 2) + anchor_z - depth
    inside = (
        (coord_x >= 0)
        & (coord_x < whole_x)
        & (coord_y >= 0)
        & (coord_y < whole_y)
        & (coord_z >= 0)
        & (coord_z < whole_z)
    )
    margin = depth - 1
    ext_x = tile_x + 2 * margin
    ext_y = tile_y + 2 * margin
    ext_z = tile_z + 2 * margin
    local_x = receiver_cells // (whole_y * whole_z) - anchor_x + margin
    local_y = receiver_cells // whole_z % whole_y - anchor_y + margin
    local_z = receiver_cells % whole_z - anchor_z + margin
    within = (
        (local_x >= 0)
        & (local_x < ext_x)
        & (local_y >= 0)
        & (local_y < ext_y)
        & (local_z >= 0)
        & (local_z < ext_z)
    )
    ext_cells = ext_x * ext_y * ext_z
    flat_index = jnp.where(within, (local_x * ext_y + local_y) * ext_z + local_z, ext_cells)
    state = adjoint_fields
    panels = []
    for block in range(moments // depth):
        padded = padded_2(state, (("gx", 2), ("gy", 3), ("gz", 4)), 1)
        moment = block * depth
        electric = padded[0:3]
        magnetic = padded[3:6]
        tile_e = crop(electric, depth, 0)
        forward_f = forward_fields[moment].astype(jnp.float32)
        panels.append(
            sigma_tile
            * (forward_f[0] * tile_e[0] + forward_f[1] * tile_e[1] + forward_f[2] * tile_e[2])
        )
        electric_base = electric[:, :, :-1, :-1, :-1]
        magnetic_base = magnetic[:, :, :-1, :-1, :-1]
        along_x = electric[:, :, 1:, :-1, :-1] - electric_base
        along_y = electric[:, :, :-1, 1:, :-1] - electric_base
        along_z = electric[:, :, :-1, :-1, 1:] - electric_base
        new_h = jnp.stack(
            [
                magnetic_base[0] - COURANT * (along_y[2] - along_z[1]),
                magnetic_base[1] - COURANT * (along_z[0] - along_x[2]),
                magnetic_base[2] - COURANT * (along_x[1] - along_y[0]),
            ]
        )
        h_mask = crop(inside, depth, depth)[:-1, :-1, :-1]
        new_h = jnp.where(h_mask, new_h, 0.0)
        inner_h = new_h[:, :, 1:, 1:, 1:]
        back_x = inner_h - new_h[:, :, :-1, 1:, 1:]
        back_y = inner_h - new_h[:, :, 1:, :-1, 1:]
        back_z = inner_h - new_h[:, :, 1:, 1:, :-1]
        inject_ext = (
            jnp.zeros((sources, ext_cells), jnp.float32)
            .at[:, flat_index]
            .add(residuals[moment], mode="drop")
        )
        inject_ext = inject_ext.reshape(sources, ext_x, ext_y, ext_z)
        inject = crop(inject_ext, margin, depth - 1)
        keep_rate = crop(keep_ext, margin, depth - 1)
        drive_rate = crop(drive_ext, margin, depth - 1)
        middle_e = electric[:, :, 1:-1, 1:-1, 1:-1]
        new_e = jnp.stack(
            [
                keep_rate * middle_e[0] + drive_rate * (back_y[2] - back_z[1] + inject),
                keep_rate * middle_e[1] + drive_rate * (back_z[0] - back_x[2]),
                keep_rate * middle_e[2] + drive_rate * (back_x[1] - back_y[0]),
            ]
        )
        new_e = jnp.where(crop(inside, depth, depth - 1), new_e, 0.0)
        padded = jnp.concatenate([new_e, inner_h], axis=0)
        state = padded
    panel_rows = jnp.stack(panels).reshape(moments * sources, tile_x, tile_y, tile_z)
    scale_factor = 1.0 / math.sqrt(float(moments * sources) * float(whole_x * whole_y * whole_z))
    local_w = jnp.einsum(
        "kxyz,xnyz->kn", panel_rows, model_vectors, precision=lax.Precision.HIGHEST
    )
    weights = lax.psum(local_w, ("gx", "gy", "gz"))
    normal_product = scale_factor * jnp.einsum(
        "kxyz,kn->xnyz", panel_rows, weights, precision=lax.Precision.HIGHEST
    )
    return (state, normal_product)


def solution(mesh):
    in_specs = (
        P(None, None, "gx", "gy", "gz"),
        P(None, None, None, "gx", "gy", "gz"),
        P("gx", "gy", "gz"),
        P(),
        P(),
        P(),
        P("gx", None, "gy", "gz"),
    )
    out_specs = (P(None, None, "gx", "gy", "gz"), P("gx", None, "gy", "gz"))
    return jax.shard_map(local, mesh=mesh, in_specs=in_specs, out_specs=out_specs, check_vma=False)
```

profile of v0, /device:TPU:0, one launch (start us, length us, event | category | flops | bytes accessed | tf_op | source)
XLA Modules:
  0.0 104.1 jit_solution(2446326424200641260)
XLA Ops:
  0.7 0.8 fusion.61
  1.5 4.9 %collective-permute-start = (f32[6,1,1,8,128]{4,3,2,1,0:T(8,128)S(1)}, f32[6,1,1,8,128]{4,3,2,1,0:T(8,128)S(1)}, u32[]{:S(2)}, u32[]{:S(2)}) collective-permute-start(f32[6,1,1,8,128]{4,3,2,1,0:T(8,128)S(1)} %get-tuple-element.45), channel_id=1, source_target_pairs={{0,8},{8,16},{16,24},{1,9},{9,17},{17,25},{2,10},{10,18},{18,26},{... | collective-permute-start | bytes 73736 | tf_op jit(solution)/shard_map/ppermute | solution.py:16
  6.4 1.3 %collective-permute-start.1 = (f32[6,1,1,8,128]{4,3,2,1,0:T(8,128)S(1)}, f32[6,1,1,8,128]{4,3,2,1,0:T(8,128)S(1)}, u32[]{:S(2)}, u32[]{:S(2)}) collective-permute-start(f32[6,1,1,8,128]{4,3,2,1,0:T(8,128)S(1)} %get-tuple-element.44), channel_id=1, source_target_pairs={{8,0},{16,8},{24,16},{9,1},{17,9},{25,17},{10,2},{18,10},{26,18},{... | collective-permute-start | bytes 73736 | tf_op jit(solution)/shard_map/ppermute | solution.py:19
  7.8 0.1 and_and_fusion.1
  7.9 0.1 and_and_fusion
  7.9 0.6 copy-done.4
  8.5 0.1 copy-done.1
  8.7 3.4 %collective-permute-done.1 = f32[6,1,1,8,128]{4,3,2,1,0:T(8,128)S(1)} collective-permute-done((f32[6,1,1,8,128]{4,3,2,1,0:T(8,128)S(1)}, f32[6,1,1,8,128]{4,3,2,1,0:T(8,128)S(1)}, u32[]{:S(2)}, u32[]{:S(2)}) %collective-permute-start.1) | collective-permute-done | bytes 24608 | tf_op jit(solution)/shard_map/ppermute | solution.py:19
  12.1 3.4 %collective-permute-start.2 = (f32[6,1,6,1,128]{4,3,2,1,0:T(1,128)S(1)}, f32[6,1,6,1,128]{4,3,2,1,0:T(1,128)S(1)}, u32[]{:S(2)}, u32[]{:S(2)}) collective-permute-start(f32[6,1,6,1,128]{4,3,2,1,0:T(1,128)S(1)} %get-tuple-element.36), channel_id=1, source_target_pairs={{0,4},{1,5},{2,6},{3,7},{8,12},{9,13},{10,14},{11,15},{16,20},{17,... | collective-permute-start | bytes 55304 | tf_op jit(solution)/shard_map/ppermute | solution.py:16
  15.6 1.3 %collective-permute-start.3 = (f32[6,1,6,1,128]{4,3,2,1,0:T(1,128)S(1)}, f32[6,1,6,1,128]{4,3,2,1,0:T(1,128)S(1)}, u32[]{:S(2)}, u32[]{:S(2)}) collective-permute-start(f32[6,1,6,1,128]{4,3,2,1,0:T(1,128)S(1)} %get-tuple-element.37), channel_id=1, source_target_pairs={{4,0},{5,1},{6,2},{7,3},{12,8},{13,9},{14,10},{15,11},{20,16},{21,... | collective-permute-start | bytes 55304 | tf_op jit(solution)/shard_map/ppermute | solution.py:19
  16.9 0.1 collective-permute-done.2
  17.0 4.2 %collective-permute-done.3 = f32[6,1,6,1,128]{4,3,2,1,0:T(1,128)S(1)} collective-permute-done((f32[6,1,6,1,128]{4,3,2,1,0:T(1,128)S(1)}, f32[6,1,6,1,128]{4,3,2,1,0:T(1,128)S(1)}, u32[]{:S(2)}, u32[]{:S(2)}) %collective-permute-start.3) | collective-permute-done | bytes 18464 | tf_op jit(solution)/shard_map/ppermute | solution.py:19
  21.2 0.1 pad_maximum_fusion
  21.3 0.1 fusion.59
  21.5 1.3 %collective-permute-start.4 = (f32[6,1,6,10,1]{4,3,2,1,0:T(8,128)S(1)}, f32[6,1,6,10,1]{4,3,2,1,0:T(8,128)S(1)}, u32[]{:S(2)}, u32[]{:S(2)}) collective-permute-start(f32[6,1,6,10,1]{4,3,2,1,0:T(8,128)S(1)} %get-tuple-element.22), channel_id=1, source_target_pairs={{0,1},{1,2},{2,3},{4,5},{5,6},{6,7},{8,9},{9,10},{10,11},{12,13},{... | collective-permute-start | bytes 4328 | tf_op jit(solution)/shard_map/ppermute | solution.py:16
  22.8 0.1 select_reduce_fusion
  22.9 0.1 slice.401
  23.0 1.9 %scatter_custom_fusion = f32[4096]{0:T(1024)S(1)} fusion(s32[256]{0:T(256)S(1)} %compare_select_fusion, f32[256]{0:T(256)S(1)} %bitcast.93, f32[]{:T(128)} %constant.92.clone.1), kind=kCustom, calls=%fused_computation.122 | custom fusion | flops 256 | bytes 16388 | tf_op jit(solution)/shard_map/scatter-add | solution.py:122
  25.0 1.3 %collective-permute-start.5 = (f32[6,1,6,10,1]{4,3,2,1,0:T(8,128)S(1)}, f32[6,1,6,10,1]{4,3,2,1,0:T(8,128)S(1)}, u32[]{:S(2)}, u32[]{:S(2)}) collective-permute-start(f32[6,1,6,10,1]{4,3,2,1,0:T(8,128)S(1)} %get-tuple-element.21), channel_id=1, source_target_pairs={{1,0},{2,1},{3,2},{5,4},{6,5},{7,6},{9,8},{10,9},{11,10},{13,12},{... | collective-permute-start | bytes 4328 | tf_op jit(solution)/shard_map/ppermute | solution.py:19
  26.3 0.4 maximum_maximum_fusion
  26.6 3.5 %collective-permute-done.5 = f32[6,1,6,10,1]{4,3,2,1,0:T(8,128)S(1)} collective-permute-done((f32[6,1,6,10,1]{4,3,2,1,0:T(8,128)S(1)}, f32[6,1,6,10,1]{4,3,2,1,0:T(8,128)S(1)}, u32[]{:S(2)}, u32[]{:S(2)}) %collective-permute-start.5) | collective-permute-done | bytes 1472 | tf_op jit(solution)/shard_map/ppermute | solution.py:19
  30.1 0.1 fusion.2
  30.2 0.2 fusion.14
  30.5 0.1 slice_subtract_fusion.14
  30.7 3.5 %collective-permute-start.6 = (f32[6,1,1,8,128]{4,3,2,1,0:T(8,128)S(1)}, f32[6,1,1,8,128]{4,3,2,1,0:T(8,128)S(1)}, u32[]{:S(2)}, u32[]{:S(2)}) collective-permute-start(f32[6,1,1,8,128]{4,3,2,1,0:T(8,128)S(1)} %get-tuple-element.42), channel_id=1, source_target_pairs={{0,8},{8,16},{16,24},{1,9},{9,17},{17,25},{2,10},{10,18},{18,26},{... | collective-permute-start | bytes 73736 | tf_op jit(solution)/shard_map/ppermute | solution.py:16
  34.2 1.3 %collective-permute-start.7 = (f32[6,1,1,8,128]{4,3,2,1,0:T(8,128)S(1)}, f32[6,1,1,8,128]{4,3,2,1,0:T(8,128)S(1)}, u32[]{:S(2)}, u32[]{:S(2)}) collective-permute-start(f32[6,1,1,8,128]{4,3,2,1,0:T(8,128)S(1)} %get-tuple-element.43), channel_id=1, source_target_pairs={{8,0},{16,8},{24,16},{9,1},{17,9},{25,17},{10,2},{18,10},{26,18},{... | collective-permute-start | bytes 73736 | tf_op jit(solution)/shard_map/ppermute | solution.py:19
  35.5 0.2 collective-permute-done.6
  35.7 4.2 %collective-permute-done.7 = f32[6,1,1,8,128]{4,3,2,1,0:T(8,128)S(1)} collective-permute-done((f32[6,1,1,8,128]{4,3,2,1,0:T(8,128)S(1)}, f32[6,1,1,8,128]{4,3,2,1,0:T(8,128)S(1)}, u32[]{:S(2)}, u32[]{:S(2)}) %collective-permute-start.7) | collective-permute-done | bytes 24608 | tf_op jit(solution)/shard_map/ppermute | solution.py:19
  39.9 1.6 %collective-permute-start.8 = (f32[6,1,6,1,128]{4,3,2,1,0:T(1,128)S(1)}, f32[6,1,6,1,128]{4,3,2,1,0:T(1,128)S(1)}, u32[]{:S(2)}, u32[]{:S(2)}) collective-permute-start(f32[6,1,6,1,128]{4,3,2,1,0:T(1,128)S(1)} %get-tuple-element.34), channel_id=1, source_target_pairs={{0,4},{1,5},{2,6},{3,7},{8,12},{9,13},{10,14},{11,15},{16,20},{17,... | collective-permute-start | bytes 55304 | tf_op jit(solution)/shard_map/ppermute | solution.py:16
  41.6 1.3 %collective-permute-start.9 = (f32[6,1,6,1,128]{4,3,2,1,0:T(1,128)S(1)}, f32[6,1,6,1,128]{4,3,2,1,0:T(1,128)S(1)}, u32[]{:S(2)}, u32[]{:S(2)}) collective-permute-start(f32[6,1,6,1,128]{4,3,2,1,0:T(1,128)S(1)} %get-tuple-element.35), channel_id=1, source_target_pairs={{4,0},{5,1},{6,2},{7,3},{12,8},{13,9},{14,10},{15,11},{20,16},{21,... | collective-permute-start | bytes 55304 | tf_op jit(solution)/shard_map/ppermute | solution.py:19
  42.9 0.1 collective-permute-done.8
  43.0 4.2 %collective-permute-done.9 = f32[6,1,6,1,128]{4,3,2,1,0:T(1,128)S(1)} collective-permute-done((f32[6,1,6,1,128]{4,3,2,1,0:T(1,128)S(1)}, f32[6,1,6,1,128]{4,3,2,1,0:T(1,128)S(1)}, u32[]{:S(2)}, u32[]{:S(2)}) %collective-permute-start.9) | collective-permute-done | bytes 18464 | tf_op jit(solution)/shard_map/ppermute | solution.py:19
  47.2 0.1 pad_maximum_fusion.1
  47.3 0.1 fusion.58
  47.4 4.1 %collective-permute-start.10 = (f32[6,1,6,10,1]{4,3,2,1,0:T(8,128)S(1)}, f32[6,1,6,10,1]{4,3,2,1,0:T(8,128)S(1)}, u32[]{:S(2)}, u32[]{:S(2)}) collective-permute-start(f32[6,1,6,10,1]{4,3,2,1,0:T(8,128)S(1)} %get-tuple-element.20), channel_id=1, source_target_pairs={{0,1},{1,2},{2,3},{4,5},{5,6},{6,7},{8,9},{9,10},{10,11},{12,13},{... | collective-permute-start | bytes 4328 | tf_op jit(solution)/shard_map/ppermute | solution.py:16
  51.6 1.9 %scatter_custom_fusion.1 = f32[4096]{0:T(1024)S(1)} fusion(s32[256]{0:T(256)S(1)} %compare_select_fusion, f32[256]{0:T(256)S(1)} %bitcast.92, f32[]{:T(128)} %constant.92.clone.1), kind=kCustom, calls=%fused_computation.120 | custom fusion | flops 256 | bytes 16388 | tf_op jit(solution)/shard_map/scatter-add | solution.py:122
  53.5 1.3 %collective-permute-start.11 = (f32[6,1,6,10,1]{4,3,2,1,0:T(8,128)S(1)}, f32[6,1,6,10,1]{4,3,2,1,0:T(8,128)S(1)}, u32[]{:S(2)}, u32[]{:S(2)}) collective-permute-start(f32[6,1,6,10,1]{4,3,2,1,0:T(8,128)S(1)} %get-tuple-element.19), channel_id=1, source_target_pairs={{1,0},{2,1},{3,2},{5,4},{6,5},{7,6},{9,8},{10,9},{11,10},{13,12},{... | collective-permute-start | bytes 4328 | tf_op jit(solution)/shard_map/ppermute | solution.py:19
  54.8 0.4 maximum_maximum_fusion.1
  55.2 4.0 %collective-permute-done.11 = f32[6,1,6,10,1]{4,3,2,1,0:T(8,128)S(1)} collective-permute-done((f32[6,1,6,10,1]{4,3,2,1,0:T(8,128)S(1)}, f32[6,1,6,10,1]{4,3,2,1,0:T(8,128)S(1)}, u32[]{:S(2)}, u32[]{:S(2)}) %collective-permute-start.11) | collective-permute-done | bytes 1472 | tf_op jit(solution)/shard_map/ppermute | solution.py:19
  59.2 0.1 fusion.1
  59.3 0.1 fusion.6
  59.4 0.2 fusion.8
  59.6 0.1 slice_subtract_fusion.11
  59.8 0.4 convolution_bitcast_fusion
  60.1 42.4 %psum.7 = f32[2,4]{1,0:T(2,128)S(1)} all-reduce(f32[2,4]{1,0:T(2,128)S(1)} %convolution_bitcast_fusion), channel_id=1, replica_groups=mesh['gx'=4,'gy'=2,'gz'=4] {'gx','gy','gz'}, use_global_device_ids=true, to_apply=%region_3.4 | all-reduce | flops 8 | bytes 64 | tf_op jit(solution)/shard_map/psum | solution.py:144
  102.5 0.3 fusion
  102.8 0.6 copy.56
  103.5 0.6 pad_maximum_fusion.11
  (35 shorter events, 0.3 us)
Async XLA Ops:
  0.6 59.1 %copy-start = (f32[4,4,8,128]{3,2,1,0:T(8,128)S(1)}, f32[4,4,8,128]{3,2,1,0:T(8,128)}, u32[]{:S(2)}) copy-start(f32[4,4,8,128]{3,2,1,0:T(8,128)} %param.13) | copy-start | bytes 196612
  0.6 7.1 %copy-start.2 = (bf16[2,3,1,4,8,128]{5,4,3,2,1,0:T(8,128)(2,1)S(1)}, bf16[2,3,1,4,8,128]{5,4,3,2,1,0:T(8,128)(2,1)}, u32[]{:S(2)}) copy-start(bf16[2,3,1,4,8,128]{5,4,3,2,1,0:T(8,128)(2,1)} %param.8) | copy-start | bytes 147460
  1.5 7.1 %collective-permute-start = (f32[6,1,1,8,128]{4,3,2,1,0:T(8,128)S(1)}, f32[6,1,1,8,128]{4,3,2,1,0:T(8,128)S(1)}, u32[]{:S(2)}, u32[]{:S(2)}) collective-permute-start(f32[6,1,1,8,128]{4,3,2,1,0:T(8,128)S(1)} %get-tuple-element.45), channel_id=1, source_target_pairs={{0,8},{8,16},{16,24},{1,9},{9,17},{17,25},{2,10},{10,18},{18,26},{... | collective-permute-start | bytes 73736 | tf_op jit(solution)/shard_map/ppermute | solution.py:16
  6.4 5.7 %collective-permute-start.1 = (f32[6,1,1,8,128]{4,3,2,1,0:T(8,128)S(1)}, f32[6,1,1,8,128]{4,3,2,1,0:T(8,128)S(1)}, u32[]{:S(2)}, u32[]{:S(2)}) collective-permute-start(f32[6,1,1,8,128]{4,3,2,1,0:T(8,128)S(1)} %get-tuple-element.44), channel_id=1, source_target_pairs={{8,0},{16,8},{24,16},{9,1},{17,9},{25,17},{10,2},{18,10},{26,18},{... | collective-permute-start | bytes 73736 | tf_op jit(solution)/shard_map/ppermute | solution.py:19
  7.7 0.9 copy-start.1
  7.9 0.7 copy-start.4
  12.1 4.7 %copy-start.5 = (s32[256]{0:T(256)S(1)}, s32[256]{0:T(256)}, u32[]{:S(2)}) copy-start(s32[256]{0:T(256)} %param.11) | copy-start | bytes 3076
  12.1 4.9 %collective-permute-start.2 = (f32[6,1,6,1,128]{4,3,2,1,0:T(1,128)S(1)}, f32[6,1,6,1,128]{4,3,2,1,0:T(1,128)S(1)}, u32[]{:S(2)}, u32[]{:S(2)}) collective-permute-start(f32[6,1,6,1,128]{4,3,2,1,0:T(1,128)S(1)} %get-tuple-element.36), channel_id=1, source_target_pairs={{0,4},{1,5},{2,6},{3,7},{8,12},{9,13},{10,14},{11,15},{16,20},{17,... | collective-permute-start | bytes 55304 | tf_op jit(solution)/shard_map/ppermute | solution.py:16
  15.6 5.7 %collective-permute-start.3 = (f32[6,1,6,1,128]{4,3,2,1,0:T(1,128)S(1)}, f32[6,1,6,1,128]{4,3,2,1,0:T(1,128)S(1)}, u32[]{:S(2)}, u32[]{:S(2)}) collective-permute-start(f32[6,1,6,1,128]{4,3,2,1,0:T(1,128)S(1)} %get-tuple-element.37), channel_id=1, source_target_pairs={{4,0},{5,1},{6,2},{7,3},{12,8},{13,9},{14,10},{15,11},{20,16},{21,... | collective-permute-start | bytes 55304 | tf_op jit(solution)/shard_map/ppermute | solution.py:19
  21.3 1.5 %copy-start.3 = (s32[4,8,128]{2,1,0:T(8,128)S(1)}, s32[4,8,128]{2,1,0:T(8,128)}, u32[]{:S(2)}) copy-start(s32[4,8,128]{2,1,0:T(8,128)} %param.9) | copy-start | bytes 49156
  21.5 1.3 %copy-start.6 = (s32[32]{0:T(128)S(1)}, s32[32]{0:T(128)}, u32[]{:S(2)}) copy-start(s32[32]{0:T(128)} %param.10) | copy-start | bytes 388
  21.5 4.8 %collective-permute-start.4 = (f32[6,1,6,10,1]{4,3,2,1,0:T(8,128)S(1)}, f32[6,1,6,10,1]{4,3,2,1,0:T(8,128)S(1)}, u32[]{:S(2)}, u32[]{:S(2)}) collective-permute-start(f32[6,1,6,10,1]{4,3,2,1,0:T(8,128)S(1)} %get-tuple-element.22), channel_id=1, source_target_pairs={{0,1},{1,2},{2,3},{4,5},{5,6},{6,7},{8,9},{9,10},{10,11},{12,13},{... | collective-permute-start | bytes 4328 | tf_op jit(solution)/shard_map/ppermute | solution.py:16
  25.0 5.2 %collective-permute-start.5 = (f32[6,1,6,10,1]{4,3,2,1,0:T(8,128)S(1)}, f32[6,1,6,10,1]{4,3,2,1,0:T(8,128)S(1)}, u32[]{:S(2)}, u32[]{:S(2)}) collective-permute-start(f32[6,1,6,10,1]{4,3,2,1,0:T(8,128)S(1)} %get-tuple-element.21), channel_id=1, source_target_pairs={{1,0},{2,1},{3,2},{5,4},{6,5},{7,6},{9,8},{10,9},{11,10},{13,12},{... | collective-permute-start | bytes 4328 | tf_op jit(solution)/shard_map/ppermute | solution.py:19
  30.7 5.0 %collective-permute-start.6 = (f32[6,1,1,8,128]{4,3,2,1,0:T(8,128)S(1)}, f32[6,1,1,8,128]{4,3,2,1,0:T(8,128)S(1)}, u32[]{:S(2)}, u32[]{:S(2)}) collective-permute-start(f32[6,1,1,8,128]{4,3,2,1,0:T(8,128)S(1)} %get-tuple-element.42), channel_id=1, source_target_pairs={{0,8},{8,16},{16,24},{1,9},{9,17},{17,25},{2,10},{10,18},{18,26},{... | collective-permute-start | bytes 73736 | tf_op jit(solution)/shard_map/ppermute | solution.py:16
  34.2 5.7 %collective-permute-start.7 = (f32[6,1,1,8,128]{4,3,2,1,0:T(8,128)S(1)}, f32[6,1,1,8,128]{4,3,2,1,0:T(8,128)S(1)}, u32[]{:S(2)}, u32[]{:S(2)}) collective-permute-start(f32[6,1,1,8,128]{4,3,2,1,0:T(8,128)S(1)} %get-tuple-element.43), channel_id=1, source_target_pairs={{8,0},{16,8},{24,16},{9,1},{17,9},{25,17},{10,2},{18,10},{26,18},{... | collective-permute-start | bytes 73736 | tf_op jit(solution)/shard_map/ppermute | solution.py:19
  39.9 3.1 %collective-permute-start.8 = (f32[6,1,6,1,128]{4,3,2,1,0:T(1,128)S(1)}, f32[6,1,6,1,128]{4,3,2,1,0:T(1,128)S(1)}, u32[]{:S(2)}, u32[]{:S(2)}) collective-permute-start(f32[6,1,6,1,128]{4,3,2,1,0:T(1,128)S(1)} %get-tuple-element.34), channel_id=1, source_target_pairs={{0,4},{1,5},{2,6},{3,7},{8,12},{9,13},{10,14},{11,15},{16,20},{17,... | collective-permute-start | bytes 55304 | tf_op jit(solution)/shard_map/ppermute | solution.py:16
  41.6 5.7 %collective-permute-start.9 = (f32[6,1,6,1,128]{4,3,2,1,0:T(1,128)S(1)}, f32[6,1,6,1,128]{4,3,2,1,0:T(1,128)S(1)}, u32[]{:S(2)}, u32[]{:S(2)}) collective-permute-start(f32[6,1,6,1,128]{4,3,2,1,0:T(1,128)S(1)} %get-tuple-element.35), channel_id=1, source_target_pairs={{4,0},{5,1},{6,2},{7,3},{12,8},{13,9},{14,10},{15,11},{20,16},{21,... | collective-permute-start | bytes 55304 | tf_op jit(solution)/shard_map/ppermute | solution.py:19
  47.4 7.4 %collective-permute-start.10 = (f32[6,1,6,10,1]{4,3,2,1,0:T(8,128)S(1)}, f32[6,1,6,10,1]{4,3,2,1,0:T(8,128)S(1)}, u32[]{:S(2)}, u32[]{:S(2)}) collective-permute-start(f32[6,1,6,10,1]{4,3,2,1,0:T(8,128)S(1)} %get-tuple-element.20), channel_id=1, source_target_pairs={{0,1},{1,2},{2,3},{4,5},{5,6},{6,7},{8,9},{9,10},{10,11},{12,13},{... | collective-permute-start | bytes 4328 | tf_op jit(solution)/shard_map/ppermute | solution.py:16
  53.5 5.7 %collective-permute-start.11 = (f32[6,1,6,10,1]{4,3,2,1,0:T(8,128)S(1)}, f32[6,1,6,10,1]{4,3,2,1,0:T(8,128)S(1)}, u32[]{:S(2)}, u32[]{:S(2)}) collective-permute-start(f32[6,1,6,10,1]{4,3,2,1,0:T(8,128)S(1)} %get-tuple-element.19), channel_id=1, source_target_pairs={{1,0},{2,1},{3,2},{5,4},{6,5},{7,6},{9,8},{10,9},{11,10},{13,12},{... | collective-permute-start | bytes 4328 | tf_op jit(solution)/shard_map/ppermute | solution.py:19
where the time goes:
time: 105 us; the launch traced here: 104 us
  blocking collectives  42.4 us (40%)
  starting transfers between devices  26.6 us (25%)
  waiting for transfers between devices  24 us (23%)
  other arithmetic  6.79 us (6%)
  local copies, waits for them, and re-layouts  2.56 us (2%)
  between operations  1.06 us (1%)
    psum x1, blocking collectives, local(): weights = lax.psum(local_w, ('gx', 'gy', 'gz'))  42.4 us
    ppermute x6, waiting for transfers between devices, padded_2(): lax.ppermute(lax.slice_in_dim(block, 0, width, axis=dim), axis, backward)  23.6 us
    ppermute x6, starting transfers between devices, padded_2(): lax.ppermute(lax.slice_in_dim(block, block.shape[dim] - width, None, axis...  18.9 us
    ppermute x6, starting transfers between devices, padded_2(): lax.ppermute(lax.slice_in_dim(block, 0, width, axis=dim), axis, backward)  7.75 us
    scatter-add x2, other arithmetic, local(): inject_ext = jnp.zeros((sources, ext_cells), jnp.float32).at[:, flat_inde...  3.88 us
  transfers between devices with their start and end apart: 12, of which 9 were waited for; matrix products, arithmetic and copies ran while one was open for 5% of the time, Pallas kernels for 0%

commit v1 on v0

--- a/solution.py
+++ b/solution.py
@@ -141,7 +141,7 @@
     local_w = jnp.einsum(
         "kxyz,xnyz->kn", panel_rows, model_vectors, precision=lax.Precision.HIGHEST
     )
-    weights = lax.psum(local_w, ("gx", "gy", "gz"))
+    weights = lax.psum(lax.psum(local_w, ("gy", "gz")), "gx")
     normal_product = scale_factor * jnp.einsum(
         "kxyz,kn->xnyz", panel_rows, weights, precision=lax.Precision.HIGHEST
     )

time: 105 us -> 89.1 us (0.85)
  blocking collectives: 42.4 us -> 26.8 us
    psum x1 -> x2, blocking collectives: 42.4 us -> 26.8 us  [local(): weights = lax.psum(lax.psum(local_w, ('gy', 'gz')), 'gx')]
  transfers between devices with their start and end apart: 12 -> 12, of which waited for: 9 -> 9; matrix products, arithmetic and copies ran while one was open for 5% -> 6% of each run, Pallas kernels for 0% -> 0%
where the time goes in v1:
time: 89.1 us; the launch traced here: 88.6 us
  blocking collectives  26.8 us (30%)
  starting transfers between devices  26.6 us (30%)
  waiting for transfers between devices  24 us (27%)
  other arithmetic  6.79 us (8%)
  local copies, waits for them, and re-layouts  2.56 us (3%)
  between operations  1.06 us (1%)
    psum x2, blocking collectives, local(): weights = lax.psum(lax.psum(local_w, ('gy', 'gz')), 'gx')  26.8 us
    ppermute x6, waiting for transfers between devices, padded_2(): lax.ppermute(lax.slice_in_dim(block, 0, width, axis=dim), axis, backward)  23.6 us
    ppermute x6, starting transfers between devices, padded_2(): lax.ppermute(lax.slice_in_dim(block, block.shape[dim] - width, None, axis...  18.9 us
    ppermute x6, starting transfers between devices, padded_2(): lax.ppermute(lax.slice_in_dim(block, 0, width, axis=dim), axis, backward)  7.75 us
    scatter-add x2, other arithmetic, local(): inject_ext = jnp.zeros((sources, ext_cells), jnp.float32).at[:, flat_inde...  3.88 us
  transfers between devices with their start and end apart: 12, of which 9 were waited for; matrix products, arithmetic and copies ran while one was open for 6% of the time, Pallas kernels for 0%

profile of v1, /device:TPU:0, one launch (start us, length us, event | category | flops | bytes accessed | tf_op | source)
XLA Modules:
  0.0 88.6 jit_solution(313875202802181757)
XLA Ops:
  0.7 0.8 fusion.61
  1.5 4.9 %collective-permute-start = (f32[6,1,1,8,128]{4,3,2,1,0:T(8,128)S(1)}, f32[6,1,1,8,128]{4,3,2,1,0:T(8,128)S(1)}, u32[]{:S(2)}, u32[]{:S(2)}) collective-permute-start(f32[6,1,1,8,128]{4,3,2,1,0:T(8,128)S(1)} %get-tuple-element.45), channel_id=1, source_target_pairs={{0,8},{8,16},{16,24},{1,9},{9,17},{17,25},{2,10},{10,18},{18,26},{... | collective-permute-start | bytes 73736 | tf_op jit(solution)/shard_map/ppermute | solution.py:16
  6.4 1.3 %collective-permute-start.1 = (f32[6,1,1,8,128]{4,3,2,1,0:T(8,128)S(1)}, f32[6,1,1,8,128]{4,3,2,1,0:T(8,128)S(1)}, u32[]{:S(2)}, u32[]{:S(2)}) collective-permute-start(f32[6,1,1,8,128]{4,3,2,1,0:T(8,128)S(1)} %get-tuple-element.44), channel_id=1, source_target_pairs={{8,0},{16,8},{24,16},{9,1},{17,9},{25,17},{10,2},{18,10},{26,18},{... | collective-permute-start | bytes 73736 | tf_op jit(solution)/shard_map/ppermute | solution.py:19
  7.8 0.1 and_and_fusion.1
  7.9 0.1 and_and_fusion
  7.9 0.6 copy-done.4
  8.5 0.1 copy-done.1
  8.7 3.4 %collective-permute-done.1 = f32[6,1,1,8,128]{4,3,2,1,0:T(8,128)S(1)} collective-permute-done((f32[6,1,1,8,128]{4,3,2,1,0:T(8,128)S(1)}, f32[6,1,1,8,128]{4,3,2,1,0:T(8,128)S(1)}, u32[]{:S(2)}, u32[]{:S(2)}) %collective-permute-start.1) | collective-permute-done | bytes 24608 | tf_op jit(solution)/shard_map/ppermute | solution.py:19
  12.1 3.4 %collective-permute-start.2 = (f32[6,1,6,1,128]{4,3,2,1,0:T(1,128)S(1)}, f32[6,1,6,1,128]{4,3,2,1,0:T(1,128)S(1)}, u32[]{:S(2)}, u32[]{:S(2)}) collective-permute-start(f32[6,1,6,1,128]{4,3,2,1,0:T(1,128)S(1)} %get-tuple-element.36), channel_id=1, source_target_pairs={{0,4},{1,5},{2,6},{3,7},{8,12},{9,13},{10,14},{11,15},{16,20},{17,... | collective-permute-start | bytes 55304 | tf_op jit(solution)/shard_map/ppermute | solution.py:16
  15.6 1.3 %collective-permute-start.3 = (f32[6,1,6,1,128]{4,3,2,1,0:T(1,128)S(1)}, f32[6,1,6,1,128]{4,3,2,1,0:T(1,128)S(1)}, u32[]{:S(2)}, u32[]{:S(2)}) collective-permute-start(f32[6,1,6,1,128]{4,3,2,1,0:T(1,128)S(1)} %get-tuple-element.37), channel_id=1, source_target_pairs={{4,0},{5,1},{6,2},{7,3},{12,8},{13,9},{14,10},{15,11},{20,16},{21,... | collective-permute-start | bytes 55304 | tf_op jit(solution)/shard_map/ppermute | solution.py:19
  16.9 0.1 collective-permute-done.2
  17.0 4.2 %collective-permute-done.3 = f32[6,1,6,1,128]{4,3,2,1,0:T(1,128)S(1)} collective-permute-done((f32[6,1,6,1,128]{4,3,2,1,0:T(1,128)S(1)}, f32[6,1,6,1,128]{4,3,2,1,0:T(1,128)S(1)}, u32[]{:S(2)}, u32[]{:S(2)}) %collective-permute-start.3) | collective-permute-done | bytes 18464 | tf_op jit(solution)/shard_map/ppermute | solution.py:19
  21.3 0.1 fusion.59
  21.5 1.3 %collective-permute-start.4 = (f32[6,1,6,10,1]{4,3,2,1,0:T(8,128)S(1)}, f32[6,1,6,10,1]{4,3,2,1,0:T(8,128)S(1)}, u32[]{:S(2)}, u32[]{:S(2)}) collective-permute-start(f32[6,1,6,10,1]{4,3,2,1,0:T(8,128)S(1)} %get-tuple-element.22), channel_id=1, source_target_pairs={{0,1},{1,2},{2,3},{4,5},{5,6},{6,7},{8,9},{9,10},{10,11},{12,13},{... | collective-permute-start | bytes 4328 | tf_op jit(solution)/shard_map/ppermute | solution.py:16
  22.8 0.1 select_reduce_fusion
  22.9 0.1 slice.401
  23.0 1.9 %scatter_custom_fusion = f32[4096]{0:T(1024)S(1)} fusion(s32[256]{0:T(256)S(1)} %compare_select_fusion, f32[256]{0:T(256)S(1)} %bitcast.93, f32[]{:T(128)} %constant.92.clone.1), kind=kCustom, calls=%fused_computation.122 | custom fusion | flops 256 | bytes 16388 | tf_op jit(solution)/shard_map/scatter-add | solution.py:122
  25.0 1.3 %collective-permute-start.5 = (f32[6,1,6,10,1]{4,3,2,1,0:T(8,128)S(1)}, f32[6,1,6,10,1]{4,3,2,1,0:T(8,128)S(1)}, u32[]{:S(2)}, u32[]{:S(2)}) collective-permute-start(f32[6,1,6,10,1]{4,3,2,1,0:T(8,128)S(1)} %get-tuple-element.21), channel_id=1, source_target_pairs={{1,0},{2,1},{3,2},{5,4},{6,5},{7,6},{9,8},{10,9},{11,10},{13,12},{... | collective-permute-start | bytes 4328 | tf_op jit(solution)/shard_map/ppermute | solution.py:19
  26.3 0.4 maximum_maximum_fusion
  26.6 3.5 %collective-permute-done.5 = f32[6,1,6,10,1]{4,3,2,1,0:T(8,128)S(1)} collective-permute-done((f32[6,1,6,10,1]{4,3,2,1,0:T(8,128)S(1)}, f32[6,1,6,10,1]{4,3,2,1,0:T(8,128)S(1)}, u32[]{:S(2)}, u32[]{:S(2)}) %collective-permute-start.5) | collective-permute-done | bytes 1472 | tf_op jit(solution)/shard_map/ppermute | solution.py:19
  30.1 0.1 fusion.2
  30.2 0.2 fusion.14
  30.5 0.1 slice_subtract_fusion.14
  30.7 3.5 %collective-permute-start.6 = (f32[6,1,1,8,128]{4,3,2,1,0:T(8,128)S(1)}, f32[6,1,1,8,128]{4,3,2,1,0:T(8,128)S(1)}, u32[]{:S(2)}, u32[]{:S(2)}) collective-permute-start(f32[6,1,1,8,128]{4,3,2,1,0:T(8,128)S(1)} %get-tuple-element.42), channel_id=1, source_target_pairs={{0,8},{8,16},{16,24},{1,9},{9,17},{17,25},{2,10},{10,18},{18,26},{... | collective-permute-start | bytes 73736 | tf_op jit(solution)/shard_map/ppermute | solution.py:16
  34.2 1.3 %collective-permute-start.7 = (f32[6,1,1,8,128]{4,3,2,1,0:T(8,128)S(1)}, f32[6,1,1,8,128]{4,3,2,1,0:T(8,128)S(1)}, u32[]{:S(2)}, u32[]{:S(2)}) collective-permute-start(f32[6,1,1,8,128]{4,3,2,1,0:T(8,128)S(1)} %get-tuple-element.43), channel_id=1, source_target_pairs={{8,0},{16,8},{24,16},{9,1},{17,9},{25,17},{10,2},{18,10},{26,18},{... | collective-permute-start | bytes 73736 | tf_op jit(solution)/shard_map/ppermute | solution.py:19
  35.5 0.2 collective-permute-done.6
  35.7 4.2 %collective-permute-done.7 = f32[6,1,1,8,128]{4,3,2,1,0:T(8,128)S(1)} collective-permute-done((f32[6,1,1,8,128]{4,3,2,1,0:T(8,128)S(1)}, f32[6,1,1,8,128]{4,3,2,1,0:T(8,128)S(1)}, u32[]{:S(2)}, u32[]{:S(2)}) %collective-permute-start.7) | collective-permute-done | bytes 24608 | tf_op jit(solution)/shard_map/ppermute | solution.py:19
  39.9 1.6 %collective-permute-start.8 = (f32[6,1,6,1,128]{4,3,2,1,0:T(1,128)S(1)}, f32[6,1,6,1,128]{4,3,2,1,0:T(1,128)S(1)}, u32[]{:S(2)}, u32[]{:S(2)}) collective-permute-start(f32[6,1,6,1,128]{4,3,2,1,0:T(1,128)S(1)} %get-tuple-element.34), channel_id=1, source_target_pairs={{0,4},{1,5},{2,6},{3,7},{8,12},{9,13},{10,14},{11,15},{16,20},{17,... | collective-permute-start | bytes 55304 | tf_op jit(solution)/shard_map/ppermute | solution.py:16
  41.6 1.3 %collective-permute-start.9 = (f32[6,1,6,1,128]{4,3,2,1,0:T(1,128)S(1)}, f32[6,1,6,1,128]{4,3,2,1,0:T(1,128)S(1)}, u32[]{:S(2)}, u32[]{:S(2)}) collective-permute-start(f32[6,1,6,1,128]{4,3,2,1,0:T(1,128)S(1)} %get-tuple-element.35), channel_id=1, source_target_pairs={{4,0},{5,1},{6,2},{7,3},{12,8},{13,9},{14,10},{15,11},{20,16},{21,... | collective-permute-start | bytes 55304 | tf_op jit(solution)/shard_map/ppermute | solution.py:19
  42.9 0.1 collective-permute-done.8
  43.0 4.2 %collective-permute-done.9 = f32[6,1,6,1,128]{4,3,2,1,0:T(1,128)S(1)} collective-permute-done((f32[6,1,6,1,128]{4,3,2,1,0:T(1,128)S(1)}, f32[6,1,6,1,128]{4,3,2,1,0:T(1,128)S(1)}, u32[]{:S(2)}, u32[]{:S(2)}) %collective-permute-start.9) | collective-permute-done | bytes 18464 | tf_op jit(solution)/shard_map/ppermute | solution.py:19
  47.2 0.1 pad_maximum_fusion.1
  47.3 0.1 fusion.58
  47.4 4.1 %collective-permute-start.10 = (f32[6,1,6,10,1]{4,3,2,1,0:T(8,128)S(1)}, f32[6,1,6,10,1]{4,3,2,1,0:T(8,128)S(1)}, u32[]{:S(2)}, u32[]{:S(2)}) collective-permute-start(f32[6,1,6,10,1]{4,3,2,1,0:T(8,128)S(1)} %get-tuple-element.20), channel_id=1, source_target_pairs={{0,1},{1,2},{2,3},{4,5},{5,6},{6,7},{8,9},{9,10},{10,11},{12,13},{... | collective-permute-start | bytes 4328 | tf_op jit(solution)/shard_map/ppermute | solution.py:16
  51.6 1.9 %scatter_custom_fusion.1 = f32[4096]{0:T(1024)S(1)} fusion(s32[256]{0:T(256)S(1)} %compare_select_fusion, f32[256]{0:T(256)S(1)} %bitcast.92, f32[]{:T(128)} %constant.92.clone.1), kind=kCustom, calls=%fused_computation.120 | custom fusion | flops 256 | bytes 16388 | tf_op jit(solution)/shard_map/scatter-add | solution.py:122
  53.5 1.3 %collective-permute-start.11 = (f32[6,1,6,10,1]{4,3,2,1,0:T(8,128)S(1)}, f32[6,1,6,10,1]{4,3,2,1,0:T(8,128)S(1)}, u32[]{:S(2)}, u32[]{:S(2)}) collective-permute-start(f32[6,1,6,10,1]{4,3,2,1,0:T(8,128)S(1)} %get-tuple-element.19), channel_id=1, source_target_pairs={{1,0},{2,1},{3,2},{5,4},{6,5},{7,6},{9,8},{10,9},{11,10},{13,12},{... | collective-permute-start | bytes 4328 | tf_op jit(solution)/shard_map/ppermute | solution.py:19
  54.8 0.4 maximum_maximum_fusion.1
  55.2 4.0 %collective-permute-done.11 = f32[6,1,6,10,1]{4,3,2,1,0:T(8,128)S(1)} collective-permute-done((f32[6,1,6,10,1]{4,3,2,1,0:T(8,128)S(1)}, f32[6,1,6,10,1]{4,3,2,1,0:T(8,128)S(1)}, u32[]{:S(2)}, u32[]{:S(2)}) %collective-permute-start.11) | collective-permute-done | bytes 1472 | tf_op jit(solution)/shard_map/ppermute | solution.py:19
  59.2 0.1 fusion.1
  59.3 0.1 fusion.6
  59.4 0.2 fusion.8
  59.6 0.1 slice_subtract_fusion.11
  59.8 0.4 convolution_bitcast_fusion
  60.1 16.9 %psum.14 = f32[2,4]{1,0:T(2,128)S(1)} all-reduce(f32[2,4]{1,0:T(2,128)S(1)} %convolution_bitcast_fusion), channel_id=1, replica_groups=mesh['gx'=4,'gy'=2,'gz'=4] {'gy','gz'}, use_global_device_ids=true, to_apply=%region_3.4 | all-reduce | flops 8 | bytes 64 | tf_op jit(solution)/shard_map/psum | solution.py:144
  77.0 9.9 %psum.15 = f32[2,4]{1,0:T(2,128)S(1)} all-reduce(f32[2,4]{1,0:T(2,128)S(1)} %psum.14), channel_id=1, replica_groups=mesh['gx'=4,'gy'=2,'gz'=4] {'gx'}, use_global_device_ids=true, to_apply=%region_4.5 | all-reduce | flops 8 | bytes 64 | tf_op jit(solution)/shard_map/psum | solution.py:144
  86.9 0.3 fusion
  87.3 0.6 copy.56
  87.9 0.6 pad_maximum_fusion.11
  (36 shorter events, 0.4 us)
Async XLA Ops:
  0.6 59.1 %copy-start = (f32[4,4,8,128]{3,2,1,0:T(8,128)S(1)}, f32[4,4,8,128]{3,2,1,0:T(8,128)}, u32[]{:S(2)}) copy-start(f32[4,4,8,128]{3,2,1,0:T(8,128)} %param.13) | copy-start | bytes 196612
  0.6 7.1 %copy-start.2 = (bf16[2,3,1,4,8,128]{5,4,3,2,1,0:T(8,128)(2,1)S(1)}, bf16[2,3,1,4,8,128]{5,4,3,2,1,0:T(8,128)(2,1)}, u32[]{:S(2)}) copy-start(bf16[2,3,1,4,8,128]{5,4,3,2,1,0:T(8,128)(2,1)} %param.8) | copy-start | bytes 147460
  1.5 7.1 %collective-permute-start = (f32[6,1,1,8,128]{4,3,2,1,0:T(8,128)S(1)}, f32[6,1,1,8,128]{4,3,2,1,0:T(8,128)S(1)}, u32[]{:S(2)}, u32[]{:S(2)}) collective-permute-start(f32[6,1,1,8,128]{4,3,2,1,0:T(8,128)S(1)} %get-tuple-element.45), channel_id=1, source_target_pairs={{0,8},{8,16},{16,24},{1,9},{9,17},{17,25},{2,10},{10,18},{18,26},{... | collective-permute-start | bytes 73736 | tf_op jit(solution)/shard_map/ppermute | solution.py:16
  6.4 5.7 %collective-permute-start.1 = (f32[6,1,1,8,128]{4,3,2,1,0:T(8,128)S(1)}, f32[6,1,1,8,128]{4,3,2,1,0:T(8,128)S(1)}, u32[]{:S(2)}, u32[]{:S(2)}) collective-permute-start(f32[6,1,1,8,128]{4,3,2,1,0:T(8,128)S(1)} %get-tuple-element.44), channel_id=1, source_target_pairs={{8,0},{16,8},{24,16},{9,1},{17,9},{25,17},{10,2},{18,10},{26,18},{... | collective-permute-start | bytes 73736 | tf_op jit(solution)/shard_map/ppermute | solution.py:19
  7.7 0.9 %copy-start.1 = (f32[6,1,4,8,128]{4,3,2,1,0:T(8,128)S(1)}, f32[6,1,4,8,128]{4,3,2,1,0:T(8,128)}, u32[]{:S(2)}) copy-start(f32[6,1,4,8,128]{4,3,2,1,0:T(8,128)} %param.7) | copy-start | bytes 294916
  7.9 0.7 copy-start.4
  12.1 4.7 %copy-start.5 = (s32[256]{0:T(256)S(1)}, s32[256]{0:T(256)}, u32[]{:S(2)}) copy-start(s32[256]{0:T(256)} %param.11) | copy-start | bytes 3076
  12.1 4.9 %collective-permute-start.2 = (f32[6,1,6,1,128]{4,3,2,1,0:T(1,128)S(1)}, f32[6,1,6,1,128]{4,3,2,1,0:T(1,128)S(1)}, u32[]{:S(2)}, u32[]{:S(2)}) collective-permute-start(f32[6,1,6,1,128]{4,3,2,1,0:T(1,128)S(1)} %get-tuple-element.36), channel_id=1, source_target_pairs={{0,4},{1,5},{2,6},{3,7},{8,12},{9,13},{10,14},{11,15},{16,20},{17,... | collective-permute-start | bytes 55304 | tf_op jit(solution)/shard_map/ppermute | solution.py:16
  15.6 5.7 %collective-permute-start.3 = (f32[6,1,6,1,128]{4,3,2,1,0:T(1,128)S(1)}, f32[6,1,6,1,128]{4,3,2,1,0:T(1,128)S(1)}, u32[]{:S(2)}, u32[]{:S(2)}) collective-permute-start(f32[6,1,6,1,128]{4,3,2,1,0:T(1,128)S(1)} %get-tuple-element.37), channel_id=1, source_target_pairs={{4,0},{5,1},{6,2},{7,3},{12,8},{13,9},{14,10},{15,11},{20,16},{21,... | collective-permute-start | bytes 55304 | tf_op jit(solution)/shard_map/ppermute | solution.py:19
  21.3 1.5 %copy-start.3 = (s32[4,8,128]{2,1,0:T(8,128)S(1)}, s32[4,8,128]{2,1,0:T(8,128)}, u32[]{:S(2)}) copy-start(s32[4,8,128]{2,1,0:T(8,128)} %param.9) | copy-start | bytes 49156
  21.5 1.3 %copy-start.6 = (s32[32]{0:T(128)S(1)}, s32[32]{0:T(128)}, u32[]{:S(2)}) copy-start(s32[32]{0:T(128)} %param.10) | copy-start | bytes 388
  21.5 4.8 %collective-permute-start.4 = (f32[6,1,6,10,1]{4,3,2,1,0:T(8,128)S(1)}, f32[6,1,6,10,1]{4,3,2,1,0:T(8,128)S(1)}, u32[]{:S(2)}, u32[]{:S(2)}) collective-permute-start(f32[6,1,6,10,1]{4,3,2,1,0:T(8,128)S(1)} %get-tuple-element.22), channel_id=1, source_target_pairs={{0,1},{1,2},{2,3},{4,5},{5,6},{6,7},{8,9},{9,10},{10,11},{12,13},{... | collective-permute-start | bytes 4328 | tf_op jit(solution)/shard_map/ppermute | solution.py:16
  25.0 5.2 %collective-permute-start.5 = (f32[6,1,6,10,1]{4,3,2,1,0:T(8,128)S(1)}, f32[6,1,6,10,1]{4,3,2,1,0:T(8,128)S(1)}, u32[]{:S(2)}, u32[]{:S(2)}) collective-permute-start(f32[6,1,6,10,1]{4,3,2,1,0:T(8,128)S(1)} %get-tuple-element.21), channel_id=1, source_target_pairs={{1,0},{2,1},{3,2},{5,4},{6,5},{7,6},{9,8},{10,9},{11,10},{13,12},{... | collective-permute-start | bytes 4328 | tf_op jit(solution)/shard_map/ppermute | solution.py:19
  30.7 5.0 %collective-permute-start.6 = (f32[6,1,1,8,128]{4,3,2,1,0:T(8,128)S(1)}, f32[6,1,1,8,128]{4,3,2,1,0:T(8,128)S(1)}, u32[]{:S(2)}, u32[]{:S(2)}) collective-permute-start(f32[6,1,1,8,128]{4,3,2,1,0:T(8,128)S(1)} %get-tuple-element.42), channel_id=1, source_target_pairs={{0,8},{8,16},{16,24},{1,9},{9,17},{17,25},{2,10},{10,18},{18,26},{... | collective-permute-start | bytes 73736 | tf_op jit(solution)/shard_map/ppermute | solution.py:16
  34.2 5.7 %collective-permute-start.7 = (f32[6,1,1,8,128]{4,3,2,1,0:T(8,128)S(1)}, f32[6,1,1,8,128]{4,3,2,1,0:T(8,128)S(1)}, u32[]{:S(2)}, u32[]{:S(2)}) collective-permute-start(f32[6,1,1,8,128]{4,3,2,1,0:T(8,128)S(1)} %get-tuple-element.43), channel_id=1, source_target_pairs={{8,0},{16,8},{24,16},{9,1},{17,9},{25,17},{10,2},{18,10},{26,18},{... | collective-permute-start | bytes 73736 | tf_op jit(solution)/shard_map/ppermute | solution.py:19
  39.9 3.1 %collective-permute-start.8 = (f32[6,1,6,1,128]{4,3,2,1,0:T(1,128)S(1)}, f32[6,1,6,1,128]{4,3,2,1,0:T(1,128)S(1)}, u32[]{:S(2)}, u32[]{:S(2)}) collective-permute-start(f32[6,1,6,1,128]{4,3,2,1,0:T(1,128)S(1)} %get-tuple-element.34), channel_id=1, source_target_pairs={{0,4},{1,5},{2,6},{3,7},{8,12},{9,13},{10,14},{11,15},{16,20},{17,... | collective-permute-start | bytes 55304 | tf_op jit(solution)/shard_map/ppermute | solution.py:16
  41.6 5.7 %collective-permute-start.9 = (f32[6,1,6,1,128]{4,3,2,1,0:T(1,128)S(1)}, f32[6,1,6,1,128]{4,3,2,1,0:T(1,128)S(1)}, u32[]{:S(2)}, u32[]{:S(2)}) collective-permute-start(f32[6,1,6,1,128]{4,3,2,1,0:T(1,128)S(1)} %get-tuple-element.35), channel_id=1, source_target_pairs={{4,0},{5,1},{6,2},{7,3},{12,8},{13,9},{14,10},{15,11},{20,16},{21,... | collective-permute-start | bytes 55304 | tf_op jit(solution)/shard_map/ppermute | solution.py:19
  47.4 7.4 %collective-permute-start.10 = (f32[6,1,6,10,1]{4,3,2,1,0:T(8,128)S(1)}, f32[6,1,6,10,1]{4,3,2,1,0:T(8,128)S(1)}, u32[]{:S(2)}, u32[]{:S(2)}) collective-permute-start(f32[6,1,6,10,1]{4,3,2,1,0:T(8,128)S(1)} %get-tuple-element.20), channel_id=1, source_target_pairs={{0,1},{1,2},{2,3},{4,5},{5,6},{6,7},{8,9},{9,10},{10,11},{12,13},{... | collective-permute-start | bytes 4328 | tf_op jit(solution)/shard_map/ppermute | solution.py:16
  53.5 5.7 %collective-permute-start.11 = (f32[6,1,6,10,1]{4,3,2,1,0:T(8,128)S(1)}, f32[6,1,6,10,1]{4,3,2,1,0:T(8,128)S(1)}, u32[]{:S(2)}, u32[]{:S(2)}) collective-permute-start(f32[6,1,6,10,1]{4,3,2,1,0:T(8,128)S(1)} %get-tuple-element.19), channel_id=1, source_target_pairs={{1,0},{2,1},{3,2},{5,4},{6,5},{7,6},{9,8},{10,9},{11,10},{13,12},{... | collective-permute-start | bytes 4328 | tf_op jit(solution)/shard_map/ppermute | solution.py:19
